TPU v7x, 32 devices: a whole 2x2x4 slice. The times are simulated.
32 devices in a mesh: ctx: 8 (over z, x), tp: 4 (over y, core).
Axes of the slice: x: 2, y: 2, z: 4, core: 2. Of those that a mesh axis runs over, the one named last changes fastest.
Arguments:
- q_self: bfloat16 [1024, 4096], P('ctx', 'tp'), may hold values from -200 to 200
- k_self: bfloat16 [1024, 4096], P('ctx', 'tp'), may hold values from -7 to 7
- v_self: bfloat16 [1024, 4096], P('ctx', 'tp'), may hold values from -6 to 6
- window: int32 [32], replicated, may hold values from 16 to 64, as said below
- key_weight: bfloat16 [4096, 1024], P('tp'), may hold values from -0.28125 to 0.28125
- value_weight: bfloat16 [4096, 1024], P('tp'), may hold values from -0.28125 to 0.28125
- q_cross: bfloat16 [2, 1024, 4096], P(None, 'ctx', 'tp'), may hold values from -2000 to 2000
Outputs:
- self_mixed: bfloat16 [1024, 4096], P('ctx', 'tp')
- cross_mixed: bfloat16 [2, 1024, 4096], P(None, 'ctx', 'tp')
Inputs may be any that keep to these rules, and one draw needn't show every extreme that they name: Every head's window lies between 16 and 64; some head has exactly 64.
All inputs are finite; a program needn't handle non-finite values.
Results may differ from a plain program's by a relative error of at most 0.025.
Values may be sent and summed in bfloat16 or wider, within the bound.
A program may use at most 64 MiB of HBM per device.

v0:
```python
import jax
import jax.numpy as jnp
from jax import lax
from jax.sharding import PartitionSpec as P

HEAD_DIM = 128


very_low = -1e30


def from_behind(x, axis, by):
    count = lax.axis_size(axis)
    pairs = [(i, i + by) for i in range(count) if 0 <= i + by < count]
    return lax.ppermute(x, axis, pairs)


def window_attend(queries, keys, values, query_pos, key_pos, spans, scale):
    heads = spans.shape[0]
    query_heads = queries.reshape(queries.shape[0], heads, HEAD_DIM)
    key_heads = keys.reshape(keys.shape[0], heads, HEAD_DIM)
    value_heads = values.reshape(values.shape[0], heads, HEAD_DIM)
    scores = (
        jnp.einsum("qhd,khd->hqk", query_heads, key_heads, preferred_element_type=jnp.float32)
        * scale
    )
    gap = query_pos[:, None] - key_pos[None, :]
    allowed = (key_pos[None, :] >= 0) & (gap >= 0)
    allowed = allowed[None] & (gap[None] < spans[:, None, None])
    masked = jnp.where(allowed, scores, very_low)
    top = jnp.max(masked, axis=-1, keepdims=True)
    fresh = jnp.where(allowed, jnp.exp(masked - top), 0.0)
    total = jnp.sum(fresh, axis=-1)
    summed = jnp.einsum(
        "hqk,khd->qhd", fresh.astype(jnp.bfloat16), value_heads, preferred_element_type=jnp.float32
    )
    result = summed / jnp.transpose(total)[:, :, None]
    return result.reshape(queries.shape[0], heads * HEAD_DIM)


def per_device(q_self, k_self, v_self, window, key_weight, value_weight, q_cross):
    tokens = q_self.shape[0]
    stretch = tokens // 2
    devices = lax.axis_size("ctx")
    here = lax.axis_index("ctx")
    column_part = lax.axis_index("tp")
    heads_here = q_self.shape[1] // HEAD_DIM
    spans = lax.dynamic_slice_in_dim(window, column_part * heads_here, heads_here)
    scale = HEAD_DIM ** (-0.5)
    offsets = jnp.arange(stretch, dtype=jnp.int32)
    doubled = jnp.arange(2 * stretch, dtype=jnp.int32)
    early_start = here * stretch
    late_start = (2 * devices - 1 - here) * stretch
    below = from_behind((k_self[:stretch], v_self[:stretch]), "ctx", 1)
    above = from_behind((k_self[stretch:], v_self[stretch:]), "ctx", -1)
    at_middle = here == devices - 1
    late_keys = jnp.where(at_middle, k_self[:stretch], above[0])
    late_values = jnp.where(at_middle, v_self[:stretch], above[1])
    early = window_attend(
        q_self[:stretch],
        jnp.concatenate([below[0], k_self[:stretch]], axis=0),
        jnp.concatenate([below[1], v_self[:stretch]], axis=0),
        early_start + offsets,
        early_start - stretch + doubled,
        spans,
        scale,
    )
    late = window_attend(
        q_self[stretch:],
        jnp.concatenate([late_keys, k_self[stretch:]], axis=0),
        jnp.concatenate([late_values, v_self[stretch:]], axis=0),
        late_start + offsets,
        late_start - stretch + doubled,
        spans,
        scale,
    )
    self_mixed = jnp.concatenate([early, late], axis=0).astype(jnp.bfloat16)
    partial_key = jnp.dot(self_mixed, key_weight, preferred_element_type=jnp.float32)
    partial_value = jnp.dot(self_mixed, value_weight, preferred_element_type=jnp.float32)
    summed_key, summed_value = (
        lax.psum_scatter(partial_key, "tp", scatter_dimension=1, tiled=True),
        lax.psum_scatter(partial_value, "tp", scatter_dimension=1, tiled=True),
    )
    key_cache = summed_key.astype(jnp.bfloat16)
    value_cache = summed_value.astype(jnp.bfloat16)
    kv_here = key_cache.shape[1] // HEAD_DIM
    group = heads_here // kv_here
    layers = q_cross.shape[0]
    queries = q_cross.reshape(layers, 2, stretch, kv_here, group, HEAD_DIM)
    query_pos = (early_start + offsets, late_start + offsets)

    def fold_for(query_block):

        def absorb(state, side, key_rows, value_rows, key_pos):
            top, total, summed = state
            scores = (
                jnp.einsum(
                    "lcagd,kad->lagck",
                    query_block[:, side],
                    key_rows,
                    preferred_element_type=jnp.float32,
                )
                * scale
            )
            allowed = key_pos[None, :] <= query_pos[side][:, None]
            masked = jnp.where(allowed, scores, very_low)
            new_top = jnp.maximum(top, jnp.max(masked, axis=-1))
            fresh = jnp.where(allowed, jnp.exp(masked - new_top[..., None]), 0.0)
            factor = jnp.exp(top - new_top)
            new_total = total * factor + jnp.sum(fresh, axis=-1)
            added = jnp.einsum(
                "lagck,kad->lagcd",
                fresh.astype(jnp.bfloat16),
                value_rows,
                preferred_element_type=jnp.float32,
            )
            return (new_top, new_total, summed * factor[..., None] + added)

        def fold_step(carry, piece, start):
            rows = piece[0].shape[0]
            width = 512
            count = rows // width
            key_blocks = piece[0].reshape(count, width, kv_here, HEAD_DIM)
            value_blocks = piece[1].reshape(count, width, kv_here, HEAD_DIM)

            def inner(state, inputs):
                key_rows, value_rows, number = inputs
                stored = number * width + jnp.arange(width, dtype=jnp.int32)
                owner = stored // tokens
                within = stored % tokens
                stretch_id = jnp.where(within < stretch, owner, 2 * devices - 1 - owner)
                key_pos = stretch_id * stretch + within % stretch
                updated = []
                for side in range(2):
                    fresh_state = absorb(state[side], side, key_rows, value_rows, key_pos)
                    updated.append(fresh_state)
                return ((updated[0], updated[1]), None)

            result, unused = lax.scan(
                inner, carry, (key_blocks, value_blocks, jnp.arange(count, dtype=jnp.int32))
            )
            return result

        return fold_step

    top = jnp.full((layers, kv_here, group, stretch), very_low, jnp.float32)
    total = jnp.zeros((layers, kv_here, group, stretch), jnp.float32)
    summed = jnp.zeros((layers, kv_here, group, stretch, HEAD_DIM), jnp.float32)
    state = fold_for(queries)(
        ((top, total, summed), (top, total, summed)),
        (
            lax.all_gather(key_cache, "ctx", axis=0, tiled=True),
            lax.all_gather(value_cache, "ctx", axis=0, tiled=True),
        ),
        jnp.int32(0),
    )
    sides = []
    for side in range(2):
        top, total, summed = state[side]
        result = summed / total[..., None]
        result = jnp.transpose(result, (0, 3, 1, 2, 4))
        sides.append(result.reshape(result.shape[0], stretch, heads_here * HEAD_DIM))
    cross_mixed = jnp.concatenate(sides, axis=1)
    return (self_mixed, cross_mixed.astype(jnp.bfloat16))


def solution(mesh):
    placed = (
        P("ctx", "tp"),
        P("ctx", "tp"),
        P("ctx", "tp"),
        P(),
        P("tp", None),
        P("tp", None),
        P(None, "ctx", "tp"),
    )
    return jax.shard_map(
        per_device,
        mesh=mesh,
        in_specs=placed,
        out_specs=(P("ctx", "tp"), P(None, "ctx", "tp")),
        check_vma=False,
    )
```

profile of v0, /device:TPU:0, one launch (start us, length us, event | category | flops | bytes accessed | tf_op | source)
XLA Modules:
  0.0 163.6 jit_solution(15634346151353373486)
XLA Ops:
  7.2 1.1 fusion.68
  8.4 0.2 copy.38
  8.5 4.9 %collective-permute-start = (bf16[64,1024]{0,1:T(8,128)(2,1)S(1)}, bf16[64,1024]{0,1:T(8,128)(2,1)S(1)}, u32[]{:S(2)}, u32[]{:S(2)}) collective-permute-start(bf16[64,1024]{0,1:T(8,128)(2,1)S(1)} %copy.38), channel_id=1, source_target_pairs={{0,4},{4,8},{8,12},{12,16},{16,20},{20,24},{24,28},{1,5},{5,9},{9,... | collective-permute-start | bytes 393224 | tf_op jit(solution)/shard_map/ppermute | solution.py:15
  13.4 0.2 copy.40
  13.6 1.3 collective-permute-start.2
  14.9 1.0 fusion.67
  15.9 0.2 copy.39
  16.0 5.2 %collective-permute-start.1 = (bf16[64,1024]{0,1:T(8,128)(2,1)S(1)}, bf16[64,1024]{0,1:T(8,128)(2,1)}, u32[]{:S(2)}, u32[]{:S(2)}) collective-permute-start(bf16[64,1024]{0,1:T(8,128)(2,1)S(1)} %copy.39), channel_id=1, source_target_pairs={{0,4},{4,8},{8,12},{12,16},{16,20},{20,24},{24,28},{1,5},{5,9},{9,... | collective-permute-start | bytes 393224 | tf_op jit(solution)/shard_map/ppermute | solution.py:15
  21.3 0.2 copy.41
  21.5 1.3 collective-permute-start.3
  22.8 0.5 broadcast_compare_fusion.3
  23.4 0.7 broadcast_subtract_fusion
  24.1 1.6 %slice_bitcast_fusion = (bf16[8,8,8,128]{3,2,1,0:T(8,128)(2,1)}, bf16[8,8,8,128]{3,2,1,0:T(8,128)(2,1)S(1)}) fusion(bf16[128,1024]{1,0:T(8,128)(2,1)} %param.9), kind=kLoop, calls=%fused_computation.112 | loop fusion | bytes 524288
  25.8 1.3 dynamic_slice.26
  27.0 0.7 broadcast_subtract_fusion.1
  27.7 0.8 compare_and_fusion.3
  28.5 7.3 %collective-permute-done.1 = bf16[64,1024]{0,1:T(8,128)(2,1)} collective-permute-done((bf16[64,1024]{0,1:T(8,128)(2,1)S(1)}, bf16[64,1024]{0,1:T(8,128)(2,1)}, u32[]{:S(2)}, u32[]{:S(2)}) %collective-permute-start.1) | collective-permute-done | bytes 131104 | tf_op jit(solution)/shard_map/ppermute | solution.py:15
  35.8 1.8 %pad_maximum_fusion.2 = bf16[128,1024]{0,1:T(8,128)(2,1)} fusion(bf16[64,1024]{0,1:T(8,128)(2,1)S(1)} %copy.39, bf16[64,1024]{0,1:T(8,128)(2,1)} %collective-permute-done.1), kind=kLoop, calls=%fused_computation.96 | loop fusion | flops 524288 | bytes 524288 | tf_op jit(solution)/shard_map/concatenate | solution.py:61
  37.6 2.5 %fusion.69 = (f32[8,64]{1,0:T(8,128)}, bf16[8,64,128]{2,1,0:T(8,128)(2,1)}) fusion(s32[8]{0:T(128)} %dynamic_slice.26, s32[64,128]{1,0:T(8,128)} %broadcast_subtract_fusion.1, pred[64,128]{1,0:T(8,128)(4,1)S(1)} %compare_and_fusion.3, bf16[128,8,128]{0,2,1:T(8,128)(2,1)} %bitcast.163, bf16[8,8,8,128]{3,2,1,0:T(8,128)(2,1)S(1)} %get-tuple-element.327), kind=kOutput, calls=%fused_computation.127 | convolution fusion | flops 17432704 | bytes 567328 | tf_op jit(solution)/shard_map/sub | solution.py:32
  40.3 1.2 fusion.58
  41.5 1.0 broadcast_select_fusion.1
  42.5 0.1 pad_maximum_fusion.3
  42.7 1.0 broadcast_select_fusion
  43.9 1.2 fusion.70
  45.1 0.3 fusion.57
  45.4 1.2 fusion.76
  46.7 2.9 %fusion.75 = f32[128,1024]{1,0:T(8,128)} fusion(bf16[128,1024]{1,0:T(8,128)(2,1)S(1)} %bitcast_dynamic-update-slice_fusion, bf16[1024,1024]{1,0:T(8,128)(2,1)} %param.13), kind=kOutput, calls=%fused_computation.129 | convolution fusion | flops 268435456 | bytes 2883584 | tf_op jit(solution)/shard_map/dot_general | solution.py:78
  49.7 0.4 reshape.269
  50.1 0.9 copy.26
  51.0 18.8 %reduce-scatter.5.cloned.1.call-done = f32[128,256]{1,0:T(8,128)} async-done(((f32[128,1024]{1,0:T(8,128)}), f32[128,256]{1,0:T(8,128)}) %reduce-scatter.5.cloned.1.call-update) | async-done | bytes 131088 | tf_op jit(solution)/shard_map/reduce_scatter | solution.py:82
  69.9 0.9 convert_element_type.31
  70.8 31.3 %all_gather.7 = bf16[1024,256]{1,0:T(8,128)(2,1)S(1)} all-gather(bf16[128,256]{1,0:T(8,128)(2,1)S(1)} %convert_element_type.31), channel_id=1, replica_groups=mesh['ctx'=8,'tp'=4] {'ctx'}, dimensions={0}, use_global_device_ids=true | all-gather | bytes 589824 | tf_op jit(solution)/shard_map/all_gather | solution.py:153
  102.2 0.9 convert_element_type.30
  103.1 33.4 %all_gather.6 = bf16[1024,256]{1,0:T(8,128)(2,1)} all-gather(bf16[128,256]{1,0:T(8,128)(2,1)S(1)} %convert_element_type.30), channel_id=1, replica_groups=mesh['ctx'=8,'tp'=4] {'ctx'}, dimensions={0}, use_global_device_ids=true | all-gather | bytes 589824 | tf_op jit(solution)/shard_map/all_gather | solution.py:152
  136.5 1.2 reshape.268
  137.7 16.0 %while.24 = (s32[]{:T(128)}, f32[2,2,4,64]{3,2,0,1:T(4,128)S(1)}, f32[2,2,4,64]{3,2,0,1:T(4,128)S(1)}, f32[2,2,4,64,128]{4,3,2,0,1:T(8,128)}, f32[2,2,4,64]{3,2,...) while((s32[]{:T(128)}, f32[2,2,4,64]{3,2,0,1:T(4,128)S(1)}, ...), condition=%wide.region_11.12_spmd.clone, body=%wide.region_6.11_spmd.clone.sunk | while | flops 551383168 | bytes 28185952 | solution.py:139
  137.7 0.6 dynamic_slice.37
  139.0 0.2 constant_dynamic-slice_fusion.5
  139.2 0.2 constant_dynamic-slice_fusion.4
  139.4 1.5 fusion.101
  140.9 0.7 fusion.102
  141.7 0.5 fusion.100
  142.2 0.7 fusion.103
  143.0 0.8 fusion.106
  143.8 0.2 copy-done.4
  144.0 0.8 fusion.105
  144.9 0.8 copy-done.5
  145.7 0.6 dynamic_slice.37
  146.9 0.2 constant_dynamic-slice_fusion.5
  147.1 0.2 constant_dynamic-slice_fusion.4
  147.4 1.5 fusion.101
  148.9 0.7 fusion.102
  149.6 0.5 fusion.100
  150.2 0.7 fusion.103
  150.9 0.8 fusion.106
  151.8 0.2 copy-done.4
  152.0 0.8 fusion.105
  152.9 0.8 copy-done.5
  153.6 1.5 fusion.59
  155.2 0.2 copy.28
  155.4 0.2 reshape.271
  155.6 0.2 copy.29
  155.8 0.2 reshape.272
  156.0 0.8 pad_maximum_fusion
  (74 shorter events, 1.1 us)
Async XLA Ops:
  7.2 38.3 %copy-start = (bf16[1024,1024]{1,0:T(8,128)(2,1)S(1)}, bf16[1024,1024]{1,0:T(8,128)(2,1)}, u32[]{:S(2)}) copy-start(bf16[1024,1024]{1,0:T(8,128)(2,1)} %param.14) | copy-start | bytes 6291460
  7.2 62.7 %reduce-scatter.5.cloned.1.call-start = ((), (), s32[]{:S(2)}) async-start(), calls=%async_computation.3 | async-start | bytes 655360 | tf_op jit(solution)/shard_map/reduce_scatter | solution.py:82
  8.5 31.6 %collective-permute-start = (bf16[64,1024]{0,1:T(8,128)(2,1)S(1)}, bf16[64,1024]{0,1:T(8,128)(2,1)S(1)}, u32[]{:S(2)}, u32[]{:S(2)}) collective-permute-start(bf16[64,1024]{0,1:T(8,128)(2,1)S(1)} %copy.38), channel_id=1, source_target_pairs={{0,4},{4,8},{8,12},{12,16},{16,20},{20,24},{24,28},{1,5},{5,9},{9,... | collective-permute-start | bytes 393224 | tf_op jit(solution)/shard_map/ppermute | solution.py:15
  13.6 27.9 %collective-permute-start.2 = (bf16[64,1024]{0,1:T(8,128)(2,1)S(1)}, bf16[64,1024]{0,1:T(8,128)(2,1)}, u32[]{:S(2)}, u32[]{:S(2)}) collective-permute-start(bf16[64,1024]{0,1:T(8,128)(2,1)S(1)} %copy.40), channel_id=1, source_target_pairs={{4,0},{8,4},{12,8},{16,12},{20,16},{24,20},{28,24},{5,1},{9,5},{13... | collective-permute-start | bytes 393224 | tf_op jit(solution)/shard_map/ppermute | solution.py:15
  16.0 19.7 %collective-permute-start.1 = (bf16[64,1024]{0,1:T(8,128)(2,1)S(1)}, bf16[64,1024]{0,1:T(8,128)(2,1)}, u32[]{:S(2)}, u32[]{:S(2)}) collective-permute-start(bf16[64,1024]{0,1:T(8,128)(2,1)S(1)} %copy.39), channel_id=1, source_target_pairs={{0,4},{4,8},{8,12},{12,16},{16,20},{20,24},{24,28},{1,5},{5,9},{9,... | collective-permute-start | bytes 393224 | tf_op jit(solution)/shard_map/ppermute | solution.py:15
  21.5 21.2 %collective-permute-start.3 = (bf16[64,1024]{0,1:T(8,128)(2,1)S(1)}, bf16[64,1024]{0,1:T(8,128)(2,1)}, u32[]{:S(2)}, u32[]{:S(2)}) collective-permute-start(bf16[64,1024]{0,1:T(8,128)(2,1)S(1)} %copy.41), channel_id=1, source_target_pairs={{4,0},{8,4},{12,8},{16,12},{20,16},{24,20},{28,24},{5,1},{9,5},{13... | collective-permute-start | bytes 393224 | tf_op jit(solution)/shard_map/ppermute | solution.py:15
  22.8 4.3 %copy-start.9 = (s32[128]{0:T(128)}, s32[128]{0:T(128)S(1)}, u32[]{:S(2)}) copy-start(s32[128]{0:T(128)S(1)} %iota_add_fusion.6) | copy-start | bytes 1540
  23.3 3.7 %copy-start.10 = (s32[64]{0:T(128)}, s32[64]{0:T(128)S(1)}, u32[]{:S(2)}) copy-start(s32[64]{0:T(128)S(1)} %iota_add_fusion.5) | copy-start | bytes 772
  40.2 3.6 %copy-start.8 = (bf16[8,8,8,128]{3,2,1,0:T(8,128)(2,1)S(1)}, bf16[8,8,8,128]{3,2,1,0:T(8,128)(2,1)}, u32[]{:S(2)}) copy-start(bf16[8,8,8,128]{3,2,1,0:T(8,128)(2,1)} %get-tuple-element.326) | copy-start | bytes 393220
  40.3 3.6 %copy-start.11 = (s32[8]{0:T(128)S(1)}, s32[8]{0:T(128)}, u32[]{:S(2)}) copy-start(s32[8]{0:T(128)} %dynamic_slice.26) | copy-start | bytes 100
  45.4 4.2 %copy-start.1 = (bf16[128,1024]{1,0:T(8,128)(2,1)}, bf16[128,1024]{1,0:T(8,128)(2,1)S(1)}, u32[]{:S(2)}) copy-start(bf16[128,1024]{1,0:T(8,128)(2,1)S(1)} %bitcast_dynamic-update-slice_fusion) | copy-start | bytes 786436
  46.7 3.1 %copy-start.6 = (bf16[2,128,1024]{2,1,0:T(8,128)(2,1)S(1)}, bf16[2,128,1024]{2,1,0:T(8,128)(2,1)}, u32[]{:S(2)}) copy-start(bf16[2,128,1024]{2,1,0:T(8,128)(2,1)} %param.15) | copy-start | bytes 1572868
  46.7 55.5 %reduce-scatter.3.cloned.1.call-start = ((), (), s32[]{:S(2)}) async-start(), calls=%async_computation.2 | async-start | bytes 655360 | tf_op jit(solution)/shard_map/reduce_scatter | solution.py:81
  139.4 2.3 %copy-start.7 = (bf16[2,2,64,2,4,128]{5,2,4,0,3,1:T(8,128)(2,1)S(1)}, bf16[2,2,64,2,4,128]{5,2,4,0,3,1:T(8,128)(2,1)}, u32[]{:S(2)}) copy-start(bf16[2,2,64,2,4,128]{5,2,4,0,3,1:T(8,128)(2,1)} %get-tuple-element.482) | copy-start | bytes 1572868 | tf_op jit(solution)/shard_map/while
  141.7 1.3 copy-start.2
  143.0 1.0 copy-start.4
  143.8 1.0 copy-start.3
  144.9 0.8 copy-start.5
  147.3 2.3 %copy-start.7 = (bf16[2,2,64,2,4,128]{5,2,4,0,3,1:T(8,128)(2,1)S(1)}, bf16[2,2,64,2,4,128]{5,2,4,0,3,1:T(8,128)(2,1)}, u32[]{:S(2)}) copy-start(bf16[2,2,64,2,4,128]{5,2,4,0,3,1:T(8,128)(2,1)} %get-tuple-element.482) | copy-start | bytes 1572868 | tf_op jit(solution)/shard_map/while
  149.6 1.3 copy-start.2
  150.9 1.0 copy-start.4
  151.8 1.0 copy-start.3
  152.8 0.8 copy-start.5
Sparse Core Ops, SparseCore 0:
  46.8 23.0 reduce-scatter.4
  72.5 21.6 reduce-scatter.2
where the time goes:
time: 164 us
  blocking collectives  64.6 us (39%)
  waiting for transfers between devices  26.2 us (16%)
  matrix products  16.9 us (10%)
  between operations  14.4 us (9%)
  other arithmetic  14.3 us (9%)
  local copies, waits for them, and re-layouts  12.9 us (8%)
  starting transfers between devices  12.8 us (8%)
    all_gather x1, blocking collectives, per_device(): lax.all_gather(key_cache, 'ctx', axis=0, tiled=True)  33.4 us
    all_gather x1, blocking collectives, per_device(): lax.all_gather(value_cache, 'ctx', axis=0, tiled=True)  31.3 us
    reduce_scatter x1, waiting for transfers between devices, per_device(): lax.psum_scatter(partial_value, 'tp', scatter_dimension=1, tiled=True)  18.8 us
    ppermute x4, starting transfers between devices, from_behind(): return lax.ppermute(x, axis, pairs)  12.7 us
    ppermute x4, waiting for transfers between devices, from_behind(): return lax.ppermute(x, axis, pairs)  7.31 us
    dot_general x4, matrix products, absorb(): jnp.einsum('lcagd,kad->lagck', query_block[:, side], key_rows, preferred_...  4.16 us
    sub x2, matrix products, window_attend(): fresh = jnp.where(allowed, jnp.exp(masked - top), 0.0)  3.74 us
    dot_general x4, matrix products, absorb(): jnp.einsum('lagck,kad->lagcd', fresh.astype(jnp.bfloat16), value_rows, pr...  3.37 us
  transfers between devices with their start and end apart: 6, of which 2 were waited for; matrix products, arithmetic and copies ran while one was open for 12% of the time, Pallas kernels for 0%

commit v1 on v0

v1 whole, which is shorter than its diff:
```python
import functools
import math

import jax
import jax.numpy as jnp
from jax import lax
from jax.experimental import pallas as pl
from jax.experimental.pallas import tpu as pltpu
from jax.sharding import PartitionSpec as P

HEAD_DIM = 128
LOW = -1e30
MESH = pl.DeviceIdType.MESH
FACTOR = HEAD_DIM ** (-0.5) * math.log2(math.e)
NT = (((1,), (1,)), ((), ()))
TN = (((0,), (0,)), ((), ()))


def dot(a, b, dims=(((1,), (0,)), ((), ()))):
    return lax.dot_general(a, b, dims, preferred_element_type=jnp.float32)


def kernel(
    n, tpn, window, q_hbm, k_hbm, v_hbm, kw_hbm, vw_hbm, qc_hbm, self_hbm, cross_hbm,
    q, kcat, vcat, kw, vw, qc, mix, part_out, part_in, own, cache, qbuf,
    s1, s2, tops, sums, acc, out,
    load_sem, halo_send, halo_recv, rs_send, rs_recv, ag_send, ag_recv, out_sem,
):
    me = lax.axis_index("ctx")
    tp = lax.axis_index("tp")
    stretch = q.shape[0] // 2
    heads = q.shape[1] // HEAD_DIM
    layers = qc.shape[0]
    width = part_out.shape[-1] // 2
    kvh = width // HEAD_DIM
    group = heads // kvh
    rows = layers * group * stretch
    lines = n // 2
    z = me // 2
    xx = me % 2

    def load(number, src, dst):
        copy = pltpu.make_async_copy(src, dst, load_sem.at[number])
        copy.start()
        return copy

    both = [pl.ds(0, stretch), pl.ds(stretch, stretch)]
    loads = [load(0, q_hbm, q)]
    for b in range(2):
        loads.append(load(1 + b, k_hbm.at[both[b]], kcat.at[b, both[1]]))
        loads.append(load(3 + b, v_hbm.at[both[b]], vcat.at[b, both[1]]))
    load_w = [load(5, kw_hbm, kw), load(6, vw_hbm, vw)]
    load_c = load(7, qc_hbm, qc)

    barrier = pltpu.get_barrier_semaphore()
    for step in (-2, -1, 1, 2):
        ok = (me + step >= 0) & (me + step < n)

        @pl.when(ok)
        def _():
            pl.semaphore_signal(
                barrier, inc=1, device_id={"ctx": me + step, "tp": tp}, device_id_type=MESH
            )

    def flip(o):
        t = tp
        bit = 1
        while bit < tpn:
            if o & bit:
                t = t + bit - 2 * bit * ((tp // bit) % 2)
            bit *= 2
        return t

    for o in range(1, tpn):
        pl.semaphore_signal(
            barrier, inc=1, device_id={"ctx": me, "tp": flip(o)}, device_id_type=MESH
        )
    peers = tpn - 1
    for step in (1, 2):
        peers = peers + jnp.where(me >= step, 1, 0) + jnp.where(me + step < n, 1, 0)
    pl.semaphore_wait(barrier, peers)

    def halo(b, which):
        src, cat = ((k_hbm, kcat), (v_hbm, vcat))[which]
        return pltpu.make_async_remote_copy(
            src_ref=src.at[both[b]],
            dst_ref=cat.at[b, both[0]],
            send_sem=halo_send.at[b, which],
            recv_sem=halo_recv.at[b, which],
            device_id={"ctx": me + (1, -1)[b], "tp": tp},
            device_id_type=MESH,
        )

    sends_halo = (me < n - 1, me > 0)
    takes_halo = (me > 0, me < n - 1)
    for b in range(2):
        @pl.when(sends_halo[b])
        def _():
            halo(b, 0).start()
            halo(b, 1).start()

    for copy in loads:
        copy.wait()

    @pl.when(me == 0)
    def _():
        kcat[0, :stretch] = jnp.zeros((stretch, kcat.shape[2]), kcat.dtype)
        vcat[0, :stretch] = jnp.zeros((stretch, kcat.shape[2]), kcat.dtype)

    @pl.when(me == n - 1)
    def _():
        kcat[1, :stretch] = kcat[0, stretch:]
        vcat[1, :stretch] = vcat[0, stretch:]

    load_c.wait()
    for side in range(2):
        for a in range(kvh):
            for l in range(layers):
                for g in range(group):
                    at = (l * group + g) * stretch
                    h = a * group + g
                    qbuf[side, a, at : at + stretch] = qc[
                        l, side * stretch : (side + 1) * stretch, h * HEAD_DIM : (h + 1) * HEAD_DIM
                    ]

    gap = (
        lax.broadcasted_iota(jnp.int32, (stretch, 2 * stretch), 0)
        + stretch
        - lax.broadcasted_iota(jnp.int32, (stretch, 2 * stretch), 1)
    )

    def rs_copy(b, o):
        return pltpu.make_async_remote_copy(
            src_ref=part_out.at[b, o - 1],
            dst_ref=part_in.at[b, o - 1],
            send_sem=rs_send.at[b, o - 1],
            recv_sem=rs_recv.at[b, o - 1],
            device_id={"ctx": me, "tp": flip(o)},
            device_id_type=MESH,
        )

    for b in range(2):
        @pl.when(takes_halo[b])
        def _():
            halo(b, 0).wait_recv()
            halo(b, 1).wait_recv()

        if b == 0:
            most = jnp.where(me == 0, lax.broadcasted_iota(jnp.int32, gap.shape, 0), 2 * stretch)
        here = slice(b * stretch, (b + 1) * stretch)
        for h in range(heads):
            cols = slice(h * HEAD_DIM, (h + 1) * HEAD_DIM)
            s = dot(q[here, cols], kcat[b, :, cols], NT)
            allowed = (gap >= 0) & (gap < window[tp * heads + h])
            if b == 0:
                allowed = allowed & (gap <= most)
            s = jnp.where(allowed, s, LOW)
            top = jnp.max(s, axis=1, keepdims=True)
            p = jnp.exp2((s - top) * FACTOR)
            total = jnp.sum(p, axis=1, keepdims=True)
            o = dot(p.astype(jnp.bfloat16), vcat[b, :, cols])
            mix[here, cols] = (o / total).astype(jnp.bfloat16)
        if b == 0:
            for copy in load_w:
                copy.wait()
        x = mix[here, :]
        for o in [o for o in range(tpn - 1, 0, -1) if o != 1] + [1, 0]:
            if o >= tpn:
                continue
            cols = pl.ds(pl.multiple_of(flip(o) * width, HEAD_DIM), width)
            pk = dot(x, kw[:, cols])
            pv = dot(x, vw[:, cols])
            if o == 0:
                own[b, :, :width] = pk
                own[b, :, width:] = pv
            else:
                part_out[b, o - 1, :, :width] = pk.astype(jnp.bfloat16)
                part_out[b, o - 1, :, width:] = pv.astype(jnp.bfloat16)
                rs_copy(b, o).start()
    store_self = pltpu.make_async_copy(mix, self_hbm, out_sem.at[0])
    store_self.start()

    def ag_copy(part, owner, kind):
        target = (me + 2, me - 2, me + 1 - 2 * xx)[kind]
        return pltpu.make_async_remote_copy(
            src_ref=cache.at[part, owner],
            dst_ref=cache.at[part, owner],
            send_sem=ag_send.at[part, owner, kind],
            recv_sem=ag_recv.at[part, owner],
            device_id={"ctx": target, "tp": tp},
            device_id_type=MESH,
        )

    up, down = z < lines - 1, z > 0

    def plan(part, owner, where):
        if part == 0:
            if where == "own":
                return [(up, 0), (down, 1), (None, 2)]
            return [(up, 0), (None, 2)] if where == "below" else [(down, 1), (None, 2)]
        if where == "own":
            return [(down, 1), (xx == 1, 2)]
        return [(down, 1), (None, 2)]

    def act(part, owner, where, what):
        for cond, kind in plan(part, owner, where):
            if cond is None:
                getattr(ag_copy(part, owner, kind), what)()
            else:
                @pl.when(cond)
                def _():
                    getattr(ag_copy(part, owner, kind), what)()

    for b in range(2):
        value = own[b]
        for o in range(1, tpn):
            rs_copy(b, o).wait_recv()
            value = value + part_in[b, o - 1].astype(jnp.float32)
        cache[b, me] = value.astype(jnp.bfloat16)
        act(b, me, "own", "start")

    def forward(k, carry):
        @pl.when(z - k >= 0)
        def _():
            ag_copy(0, me - 2 * k, 2).wait_recv()
            act(0, me - 2 * k, "below", "start")

        @pl.when(z + k < lines)
        def _():
            for part in range(2):
                ag_copy(part, me + 2 * k, 2).wait_recv()
                act(part, me + 2 * k, "above", "start")

        return carry

    lax.fori_loop(1, lines, forward, 0)

    def collect(k, carry):
        owner = 2 * k + 1 - xx
        ag_copy(0, owner, 2).wait_recv()

        @pl.when((k > z) | ((k == z) & (xx == 0)))
        def _():
            ag_copy(1, owner, 2).wait_recv()

        return carry

    lax.fori_loop(0, lines, collect, 0)

    bunch = min(n, 8)
    deep = bunch * stretch
    slots = s1.shape[0]
    keep = (
        lax.broadcasted_iota(jnp.int32, (stretch, rows), 0)
        <= lax.broadcasted_iota(jnp.int32, (stretch, rows), 1) % stretch
    )

    def loop(count, body):
        if count <= 16:
            for i in range(count):
                body(i)
        else:
            lax.fori_loop(0, count, lambda i, c: (body(i), c)[1], 0)

    for first in range(0, kvh, slots):
        some = range(first, first + slots)
        for a in some:
            for side in range(2):
                tops[side, a] = jnp.full((1, rows), LOW, jnp.float32)
                sums[side, a] = jnp.zeros((1, rows), jnp.float32)
                acc[side, a] = jnp.zeros((HEAD_DIM, rows), jnp.float32)

        def wide_scores(i):
            for a in some:
                keys = cache[0, pl.ds(i * bunch, bunch), :, a * HEAD_DIM : (a + 1) * HEAD_DIM]
                s = dot(keys.reshape(deep, HEAD_DIM), qbuf[1, a], NT)
                s1[a - first, pl.ds(i * deep, deep)] = s
                tops[1, a] = jnp.maximum(tops[1, a], jnp.max(s, axis=0, keepdims=True))

        loop(n // bunch, wide_scores)

        def side_of(j):
            return jnp.where(j > me, 1, 0)

        def block_scores(j):
            side = side_of(j)
            free = (j != me) & (j != me + 1)
            for a in some:
                keys = cache[side, j - side, :, a * HEAD_DIM : (a + 1) * HEAD_DIM]
                s = dot(keys, qbuf[side, a], NT)
                s = jnp.where(keep | free, s, LOW)
                s2[a - first, pl.ds(j * stretch, stretch)] = s
                tops[side, a] = jnp.maximum(tops[side, a], jnp.max(s, axis=0, keepdims=True))

        loop(n + 1, block_scores)

        def wide_mix(i):
            for a in some:
                p = jnp.exp2((s1[a - first, pl.ds(i * deep, deep)] - tops[1, a]) * FACTOR)
                sums[1, a] += jnp.sum(p, axis=0, keepdims=True)
                values = cache[
                    0, pl.ds(i * bunch, bunch), :,
                    width + a * HEAD_DIM : width + (a + 1) * HEAD_DIM,
                ].reshape(deep, HEAD_DIM)
                acc[1, a] += dot(values, p.astype(jnp.bfloat16), TN)

        loop(n // bunch, wide_mix)

        def block_mix(j):
            side = side_of(j)
            for a in some:
                p = jnp.exp2((s2[a - first, pl.ds(j * stretch, stretch)] - tops[side, a]) * FACTOR)
                sums[side, a] += jnp.sum(p, axis=0, keepdims=True)
                values = cache[
                    side, j - side, :, width + a * HEAD_DIM : width + (a + 1) * HEAD_DIM
                ]
                acc[side, a] += dot(values, p.astype(jnp.bfloat16), TN)

        loop(n + 1, block_mix)

        for a in some:
            for side in range(2):
                o = (acc[side, a] / sums[side, a]).T.astype(jnp.bfloat16)
                for l in range(layers):
                    for g in range(group):
                        at = (l * group + g) * stretch
                        h = a * group + g
                        out[
                            l, side * stretch : (side + 1) * stretch,
                            h * HEAD_DIM : (h + 1) * HEAD_DIM,
                        ] = o[at : at + stretch]

    store_cross = pltpu.make_async_copy(out, cross_hbm, out_sem.at[1])
    store_cross.start()

    for b in range(2):
        @pl.when(sends_halo[b])
        def _():
            halo(b, 0).wait_send()
            halo(b, 1).wait_send()

        for o in range(1, tpn):
            rs_copy(b, o).wait_send()
        act(b, me, "own", "wait_send")

    def finish(k, carry):
        @pl.when(z - k >= 0)
        def _():
            act(0, me - 2 * k, "below", "wait_send")

        @pl.when(z + k < lines)
        def _():
            for part in range(2):
                act(part, me + 2 * k, "above", "wait_send")

        return carry

    lax.fori_loop(1, lines, finish, 0)
    store_self.wait()
    store_cross.wait()


def per_device(n, tpn, q_self, k_self, v_self, window, key_weight, value_weight, q_cross):
    tokens, columns = q_self.shape
    stretch = tokens // 2
    heads = columns // HEAD_DIM
    layers = q_cross.shape[0]
    width = key_weight.shape[1] // tpn
    kvh = width // HEAD_DIM
    rows = layers * (heads // kvh) * stretch
    slots = kvh if n <= 16 else 1
    bf, f32 = jnp.bfloat16, jnp.float32
    any_space = pl.BlockSpec(memory_space=pl.ANY)
    dma = pltpu.SemaphoreType.DMA
    return pl.pallas_call(
        functools.partial(kernel, n, tpn),
        out_shape=(
            jax.ShapeDtypeStruct(q_self.shape, bf),
            jax.ShapeDtypeStruct(q_cross.shape, bf),
        ),
        in_specs=[pl.BlockSpec(memory_space=pltpu.SMEM)] + [any_space] * 6,
        out_specs=(any_space, any_space),
        scratch_shapes=[
            pltpu.VMEM(q_self.shape, bf),
            pltpu.VMEM((2, tokens, columns), bf),
            pltpu.VMEM((2, tokens, columns), bf),
            pltpu.VMEM(key_weight.shape, bf),
            pltpu.VMEM(value_weight.shape, bf),
            pltpu.VMEM(q_cross.shape, bf),
            pltpu.VMEM(q_self.shape, bf),
            pltpu.VMEM((2, tpn - 1, stretch, 2 * width), bf),
            pltpu.VMEM((2, tpn - 1, stretch, 2 * width), bf),
            pltpu.VMEM((2, stretch, 2 * width), f32),
            pltpu.VMEM((2, n, stretch, 2 * width), bf),
            pltpu.VMEM((2, kvh, rows, HEAD_DIM), bf),
            pltpu.VMEM((slots, n * stretch, rows), f32),
            pltpu.VMEM((slots, (n + 1) * stretch, rows), f32),
            pltpu.VMEM((2, kvh, 1, rows), f32),
            pltpu.VMEM((2, kvh, 1, rows), f32),
            pltpu.VMEM((2, kvh, HEAD_DIM, rows), f32),
            pltpu.VMEM(q_cross.shape, bf),
            dma((8,)),
            dma((2, 2)),
            dma((2, 2)),
            dma((2, tpn - 1)),
            dma((2, tpn - 1)),
            dma((2, n, 3)),
            dma((2, n)),
            dma((2,)),
        ],
        compiler_params=pltpu.CompilerParams(
            collective_id=0, has_side_effects=True, vmem_limit_bytes=48 * 2**20
        ),
    )(window, q_self, k_self, v_self, key_weight, value_weight, q_cross)


def solution(mesh):
    n, tpn = mesh.shape["ctx"], mesh.shape["tp"]
    placed = (
        P("ctx", "tp"),
        P("ctx", "tp"),
        P("ctx", "tp"),
        P(),
        P("tp", None),
        P("tp", None),
        P(None, "ctx", "tp"),
    )
    return jax.shard_map(
        functools.partial(per_device, n, tpn),
        mesh=mesh,
        in_specs=placed,
        out_specs=(P("ctx", "tp"), P(None, "ctx", "tp")),
        check_vma=False,
    )
```

time: 164 us -> 52.6 us (0.32)
  blocking collectives: 64.6 us -> 0 us
  Pallas kernels: 0 us -> 44 us
  waiting for transfers between devices: 26.2 us -> 0 us
  matrix products: 16.9 us -> 0 us
  other arithmetic: 14.3 us -> 0 us
  between operations: 14.4 us -> 0.65 us
  starting transfers between devices: 12.8 us -> 0 us
  local copies, waits for them, and re-layouts: 12.9 us -> 7.63 us
    all_gather x2 -> x0, blocking collectives: 64.6 us -> none  [the longest x1 33.4 us: per_device(): lax.all_gather(key_cache, 'ctx', axis=0, tiled=True)]
    pallas_call x0 -> x1, Pallas kernels: none -> 44 us  [per_device(): pl.pallas_call(functools.partial(kernel, n, tpn), out_shape=(jax.ShapeDty...]
    reduce_scatter x2 -> x0, waiting for transfers between devices: 18.9 us -> none  [the longest x1 18.8 us: per_device(): lax.psum_scatter(partial_value, 'tp', scatter_dimension=1, tiled=True)]
    dot_general x12 -> x0, matrix products: 13.2 us -> none  [the longest x4 4.16 us: absorb(): jnp.einsum('lcagd,kad->lagck', query_block[:, side], key_rows, preferred_...]
    ppermute x4 -> x0, starting transfers between devices: 12.7 us -> none  [from_behind(): return lax.ppermute(x, axis, pairs)]
    ppermute x4 -> x0, waiting for transfers between devices: 7.31 us -> none  [from_behind(): return lax.ppermute(x, axis, pairs)]
    unnamed x21 -> x14, local copies, waits for them, and re-layouts: 3.29 us -> 7.63 us
    sub x2 -> x0, matrix products: 3.74 us -> none  [window_attend(): fresh = jnp.where(allowed, jnp.exp(masked - top), 0.0)]
  transfers between devices with their start and end apart: 6 -> 0, of which waited for: 2 -> 0; matrix products, arithmetic and copies ran while one was open for 12% -> 0% of each run, Pallas kernels for 0% -> 0%
where the time goes in v1:
time: 52.6 us; the launch traced here: 52.3 us
  Pallas kernels  44 us (84%)
  local copies, waits for them, and re-layouts  7.63 us (15%)
  between operations  0.65 us (1%)
    pallas_call x1, Pallas kernels, per_device(): pl.pallas_call(functools.partial(kernel, n, tpn), out_shape=(jax.ShapeDty...  44 us
    unnamed x14, local copies, waits for them, and re-layouts  7.63 us

profile of v1, /device:TPU:0, one launch (start us, length us, event | category | flops | bytes accessed | tf_op | source)
XLA Modules:
  0.0 52.3 jit_solution(15709366052034084001)
XLA Ops:
  0.6 0.0 copy-start
  0.6 1.6 %copy-done = bf16[1024,1024]{1,0:T(8,128)(2,1)S(1)} copy-done((bf16[1024,1024]{1,0:T(8,128)(2,1)S(1)}, bf16[1024,1024]{1,0:T(8,128)(2,1)}, u32[]{:S(2)}) %copy-start) | copy-done | bytes 2097176
  2.2 0.0 copy-start.1
  2.2 1.0 %copy-done.1 = bf16[2,128,1024]{2,1,0:T(8,128)(2,1)S(1)} copy-done((bf16[2,128,1024]{2,1,0:T(8,128)(2,1)S(1)}, bf16[2,128,1024]{2,1,0:T(8,128)(2,1)}, u32[]{:S(2)}) %copy-start.1) | copy-done | bytes 524312
  3.3 0.0 copy-start.2
  3.3 0.9 %copy-done.2 = bf16[128,1024]{1,0:T(8,128)(2,1)S(1)} copy-done((bf16[128,1024]{1,0:T(8,128)(2,1)S(1)}, bf16[128,1024]{1,0:T(8,128)(2,1)}, u32[]{:S(2)}) %copy-start.2) | copy-done | bytes 262168
  4.2 0.0 copy-start.3
  4.2 0.9 %copy-done.3 = bf16[128,1024]{1,0:T(8,128)(2,1)S(1)} copy-done((bf16[128,1024]{1,0:T(8,128)(2,1)S(1)}, bf16[128,1024]{1,0:T(8,128)(2,1)}, u32[]{:S(2)}) %copy-start.3) | copy-done | bytes 262168
  5.2 0.0 copy-start.4
  5.2 0.9 %copy-done.4 = bf16[128,1024]{1,0:T(8,128)(2,1)S(1)} copy-done((bf16[128,1024]{1,0:T(8,128)(2,1)S(1)}, bf16[128,1024]{1,0:T(8,128)(2,1)}, u32[]{:S(2)}) %copy-start.4) | copy-done | bytes 262168
  6.1 0.0 copy-start.5
  6.1 0.7 %copy-done.5 = s32[32]{0:T(128)S(1)} copy-done((s32[32]{0:T(128)S(1)}, s32[32]{0:T(128)}, u32[]{:S(2)}) %copy-start.5) | copy-done | bytes 152
  6.8 44.0 %shard_map.86 = (bf16[128,1024]{1,0:T(8,128)(2,1)S(1)}, bf16[2,128,1024]{2,1,0:T(8,128)(2,1)S(1)}) custom-call(s32[32]{0:T(128)S(1)} %copy-done.5, bf16[128,1024]{1,0:T(8,128)(2,1)S(1)} %copy-done.2, bf16[128,1024]{1,0:T(8,128)(2,1)S(1)} %copy-done.3, bf16[128,1024]{1,0:T(8,128)(2,1)S(1)} %copy-done.4, bf16[1024,1024]{1,0:T(8,128)(2,1)S(1)} %copy-done, ...), custom_call_target="tpu_custom_call" | custom-call | tf_op jit(solution)/shard_map/pallas_call | solution.py:375
  50.8 0.7 %copy.11 = bf16[128,1024]{1,0:T(8,128)(2,1)} copy(bf16[128,1024]{1,0:T(8,128)(2,1)S(1)} %get-tuple-element.4) | data formatting | bytes 524288
  51.5 0.8 %copy.12 = bf16[2,128,1024]{2,1,0:T(8,128)(2,1)} copy(bf16[2,128,1024]{2,1,0:T(8,128)(2,1)S(1)} %get-tuple-element.5) | data formatting | bytes 1048576
Async XLA Ops:
  0.6 1.6 %copy-start = (bf16[1024,1024]{1,0:T(8,128)(2,1)S(1)}, bf16[1024,1024]{1,0:T(8,128)(2,1)}, u32[]{:S(2)}) copy-start(bf16[1024,1024]{1,0:T(8,128)(2,1)} %kw_hbm.1) | copy-start | bytes 6291460
  2.2 1.0 %copy-start.1 = (bf16[2,128,1024]{2,1,0:T(8,128)(2,1)S(1)}, bf16[2,128,1024]{2,1,0:T(8,128)(2,1)}, u32[]{:S(2)}) copy-start(bf16[2,128,1024]{2,1,0:T(8,128)(2,1)} %qc_hbm.1) | copy-start | bytes 1572868
  3.3 0.9 %copy-start.2 = (bf16[128,1024]{1,0:T(8,128)(2,1)S(1)}, bf16[128,1024]{1,0:T(8,128)(2,1)}, u32[]{:S(2)}) copy-start(bf16[128,1024]{1,0:T(8,128)(2,1)} %q_hbm.1) | copy-start | bytes 786436
  4.2 0.9 %copy-start.3 = (bf16[128,1024]{1,0:T(8,128)(2,1)S(1)}, bf16[128,1024]{1,0:T(8,128)(2,1)}, u32[]{:S(2)}) copy-start(bf16[128,1024]{1,0:T(8,128)(2,1)} %k_hbm.1) | copy-start | bytes 786436
  5.2 0.9 %copy-start.4 = (bf16[128,1024]{1,0:T(8,128)(2,1)S(1)}, bf16[128,1024]{1,0:T(8,128)(2,1)}, u32[]{:S(2)}) copy-start(bf16[128,1024]{1,0:T(8,128)(2,1)} %v_hbm.1) | copy-start | bytes 786436
  6.1 0.7 %copy-start.5 = (s32[32]{0:T(128)S(1)}, s32[32]{0:T(128)}, u32[]{:S(2)}) copy-start(s32[32]{0:T(128)} %window.1) | copy-start | bytes 388

commit v2 on v1

v2 whole, which is shorter than its diff:
```python
import functools
import math

import jax
import jax.numpy as jnp
from jax import lax
from jax.experimental import pallas as pl
from jax.experimental.pallas import tpu as pltpu
from jax.sharding import PartitionSpec as P

HEAD_DIM = 128
LOW = -1e30
MESH = pl.DeviceIdType.MESH
FACTOR = HEAD_DIM ** (-0.5) * math.log2(math.e)
NT = (((1,), (1,)), ((), ()))
TN = (((0,), (0,)), ((), ()))


def dot(a, b, dims=(((1,), (0,)), ((), ()))):
    return lax.dot_general(a, b, dims, preferred_element_type=jnp.float32)


def kernel(
    n, tpn, window, q_hbm, k_hbm, v_hbm, kw_hbm, vw_hbm, qc_hbm, self_hbm, cross_hbm,
    q, kcat, vcat, kw, vw, qc, mix, part_out, part_in, own, cache, qbuf,
    tops, sums, acc, out,
    load_sem, halo_send, halo_recv, rs_send, rs_recv, line_send, cross_send, ag_recv, out_sem,
):
    me = lax.axis_index("ctx")
    tp = lax.axis_index("tp")
    stretch = q.shape[0] // 2
    heads = q.shape[1] // HEAD_DIM
    layers = qc.shape[0]
    width = part_out.shape[-1] // 2
    kvh = width // HEAD_DIM
    group = heads // kvh
    rows = layers * group * stretch
    lines = n // 2
    z = me // 2
    xx = me % 2

    def load(number, src, dst):
        copy = pltpu.make_async_copy(src, dst, load_sem.at[number])
        copy.start()
        return copy

    both = [pl.ds(0, stretch), pl.ds(stretch, stretch)]
    loads = [load(0, q_hbm, q)]
    for b in range(2):
        loads.append(load(1 + b, k_hbm.at[both[b]], kcat.at[b, both[1]]))
        loads.append(load(3 + b, v_hbm.at[both[b]], vcat.at[b, both[1]]))

    barrier = pltpu.get_barrier_semaphore()

    def greet(target):
        pl.semaphore_signal(
            barrier, inc=1, device_id={"ctx": target, "tp": tp}, device_id_type=MESH
        )

    for step in (-1, 1):
        @pl.when((me + step >= 0) & (me + step < n))
        def _():
            greet(me + step)

    def greet_line(k, carry):
        @pl.when(k != z)
        def _():
            greet(2 * k + xx)

        return carry

    lax.fori_loop(0, lines, greet_line, 0)

    def flip(o):
        t = tp
        bit = 1
        while bit < tpn:
            if o & bit:
                t = t + bit - 2 * bit * ((tp // bit) % 2)
            bit *= 2
        return t

    for o in range(1, tpn):
        pl.semaphore_signal(
            barrier, inc=1, device_id={"ctx": me, "tp": flip(o)}, device_id_type=MESH
        )
    peers = tpn - 1 + lines - 1 + jnp.where(me >= 1, 1, 0) + jnp.where(me + 1 < n, 1, 0)
    pl.semaphore_wait(barrier, peers)

    def halo(b, which):
        src, cat = ((k_hbm, kcat), (v_hbm, vcat))[which]
        return pltpu.make_async_remote_copy(
            src_ref=src.at[both[b]],
            dst_ref=cat.at[b, both[0]],
            send_sem=halo_send.at[b, which],
            recv_sem=halo_recv.at[b, which],
            device_id={"ctx": me + (1, -1)[b], "tp": tp},
            device_id_type=MESH,
        )

    sends_halo = (me < n - 1, me > 0)
    takes_halo = (me > 0, me < n - 1)
    def send_halo(b, what):
        @pl.when(sends_halo[b])
        def _():
            getattr(halo(b, 0), what)()
            getattr(halo(b, 1), what)()

    send_halo(0, "start")
    send_halo(1, "start")
    load_c = load(7, qc_hbm, qc)
    load_w = [load(5, kw_hbm, kw), load(6, vw_hbm, vw)]
    for copy in loads:
        copy.wait()

    @pl.when(me == 0)
    def _():
        kcat[0, :stretch] = jnp.zeros((stretch, kcat.shape[2]), kcat.dtype)
        vcat[0, :stretch] = jnp.zeros((stretch, kcat.shape[2]), kcat.dtype)

    @pl.when(me == n - 1)
    def _():
        kcat[1, :stretch] = kcat[0, stretch:]
        vcat[1, :stretch] = vcat[0, stretch:]

    load_c.wait()
    for side in range(2):
        for a in range(kvh):
            for l in range(layers):
                for g in range(group):
                    at = (l * group + g) * stretch
                    h = a * group + g
                    qbuf[side, a, at : at + stretch] = qc[
                        l, side * stretch : (side + 1) * stretch, h * HEAD_DIM : (h + 1) * HEAD_DIM
                    ]

    gap = (
        lax.broadcasted_iota(jnp.int32, (stretch, 2 * stretch), 0)
        + stretch
        - lax.broadcasted_iota(jnp.int32, (stretch, 2 * stretch), 1)
    )

    def rs_copy(b, o):
        return pltpu.make_async_remote_copy(
            src_ref=part_out.at[b, o - 1],
            dst_ref=part_in.at[b, o - 1],
            send_sem=rs_send.at[b, o - 1],
            recv_sem=rs_recv.at[b, o - 1],
            device_id={"ctx": me, "tp": flip(o)},
            device_id_type=MESH,
        )

    def clear(k, carry):
        cache[1, k] = jnp.zeros(cache.shape[2:], cache.dtype)
        return carry

    lax.fori_loop(0, me, clear, 0)

    def attend_self(b):
        @pl.when(takes_halo[b])
        def _():
            halo(b, 0).wait_recv()
            halo(b, 1).wait_recv()

        here = slice(b * stretch, (b + 1) * stretch)
        cols = [slice(h * HEAD_DIM, (h + 1) * HEAD_DIM) for h in range(heads)]
        base = (gap >= 0)
        if b == 0:
            own_row = lax.broadcasted_iota(jnp.int32, gap.shape, 0)
            base = base & (gap <= jnp.where(me == 0, own_row, 2 * stretch))
        s = [dot(q[here, c], kcat[b, :, c], NT) for c in cols]
        s = [
            jnp.where(base & (gap < window[tp * heads + h]), s[h], LOW) for h in range(heads)
        ]
        top = [jnp.max(t, axis=1, keepdims=True) for t in s]
        p = [jnp.exp2((t - m) * FACTOR) for t, m in zip(s, top)]
        total = [jnp.sum(t, axis=1, keepdims=True) for t in p]
        o = [dot(t.astype(jnp.bfloat16), vcat[b, :, c]) for t, c in zip(p, cols)]
        for c, t, m in zip(cols, o, total):
            mix[here, c] = (t / m).astype(jnp.bfloat16)

    def project(b):
        x = mix[b * stretch : (b + 1) * stretch, :]
        for o in [o for o in range(tpn - 1, 0, -1) if o != 1] + [1, 0]:
            if o >= tpn:
                continue
            cols = pl.ds(pl.multiple_of(flip(o) * width, HEAD_DIM), width)
            pk = dot(x, kw[:, cols])
            pv = dot(x, vw[:, cols])
            if o == 0:
                own[b, :, :width] = pk
                own[b, :, width:] = pv
            else:
                part_out[b, o - 1, :, :width] = pk.astype(jnp.bfloat16)
                part_out[b, o - 1, :, width:] = pv.astype(jnp.bfloat16)
                rs_copy(b, o).start()

    def ag_copy(part, owner, target, sem):
        return pltpu.make_async_remote_copy(
            src_ref=cache.at[part, owner],
            dst_ref=cache.at[part, owner],
            send_sem=sem,
            recv_sem=ag_recv.at[part, owner],
            device_id={"ctx": target, "tp": tp},
            device_id_type=MESH,
        )

    across = me + 1 - 2 * xx

    def line_copy(part, k):
        return ag_copy(part, me, 2 * k + xx, line_send.at[part, k])

    def cross_copy(part, k):
        return ag_copy(part, 2 * k + xx, across, cross_send.at[part, k])

    def own_cross(part, what):
        if part == 0:
            getattr(cross_copy(part, z), what)()
        else:
            @pl.when(xx == 1)
            def _():
                getattr(cross_copy(part, z), what)()

    def own_line(part, what):
        def body(i, carry):
            @pl.when(z - i >= 0)
            def _():
                getattr(line_copy(part, z - i), what)()

            if part == 0:
                @pl.when(z + i < lines)
                def _():
                    getattr(line_copy(part, z + i), what)()

            return carry

        lax.fori_loop(1, lines, body, 0)

    def gather_own(b):
        value = own[b]
        for o in range(1, tpn):
            rs_copy(b, o).wait_recv()
            value = value + part_in[b, o - 1].astype(jnp.float32)
        cache[b, me] = value.astype(jnp.bfloat16)
        own_cross(b, "start")
        own_line(b, "start")

    def forward(part, first, last):
        def body(i, carry):
            @pl.when(z + i < lines)
            def _():
                cross_copy(part, z + i).wait_recv()
                cross_copy(part, z + i).start()

            if part == 0:
                @pl.when(z - i >= 0)
                def _():
                    cross_copy(part, z - i).wait_recv()
                    cross_copy(part, z - i).start()

            return carry

        lax.fori_loop(first, last, body, 0)

    def collect(part):
        def body(k, carry):
            owner = 2 * k + 1 - xx

            def take():
                ag_copy(part, owner, across, cross_send.at[part, k]).wait_recv()

            if part == 0:
                take()
            else:
                pl.when((k > z) | ((k == z) & (xx == 0)))(take)
            return carry

        lax.fori_loop(0, lines, body, 0)

    bunch = min(n, 8)
    deep = bunch * stretch
    row = lax.broadcasted_iota(jnp.int32, (deep, rows), 0)
    keep_gap = (
        lax.broadcasted_iota(jnp.int32, (deep, rows), 1) % stretch - row % stretch
    )
    owner_of = row // stretch

    def fold(part, side, a, first):
        def body(i):
            at = pl.ds(i * bunch, bunch)
            keys = cache[part, at, :, a * HEAD_DIM : (a + 1) * HEAD_DIM]
            values = cache[part, at, :, width + a * HEAD_DIM : width + (a + 1) * HEAD_DIM]
            s = dot(keys.reshape(deep, HEAD_DIM), qbuf[side, a], NT)
            if part == side:
                ahead = me - i * bunch - owner_of
                if part == 1:
                    ahead = -ahead
                s = jnp.where((ahead > 0) | ((ahead == 0) & (keep_gap >= 0)), s, LOW)
            top = jnp.max(s, axis=0, keepdims=True)
            fresh = first and isinstance(i, int) and i == 0
            if not fresh:
                old = tops[side, a]
                top = jnp.maximum(old, top)
                factor = jnp.exp2((old - top) * FACTOR)
            p = jnp.exp2((s - top) * FACTOR)
            total = jnp.sum(p, axis=0, keepdims=True)
            added = dot(values.reshape(deep, HEAD_DIM), p.astype(jnp.bfloat16), TN)
            if not fresh:
                total = sums[side, a] * factor + total
                added = acc[side, a] * factor + added
            tops[side, a] = top
            sums[side, a] = total
            acc[side, a] = added

        count = n // bunch
        body(0)
        if count > 1:
            lax.fori_loop(1, count, lambda i, c: (body(i), c)[1], 0)

    def finish(side, a):
        o = (acc[side, a] / sums[side, a]).T.astype(jnp.bfloat16)
        for l in range(layers):
            for g in range(group):
                at = (l * group + g) * stretch
                h = a * group + g
                out[
                    l, side * stretch : (side + 1) * stretch, h * HEAD_DIM : (h + 1) * HEAD_DIM
                ] = o[at : at + stretch]

    attend_self(0)
    for copy in load_w:
        copy.wait()
    project(0)
    attend_self(1)
    store_self = pltpu.make_async_copy(mix, self_hbm, out_sem.at[0])
    store_self.start()
    gather_own(0)
    project(1)
    forward(0, 1, lines)
    gather_own(1)
    collect(0)
    for a in range(kvh):
        fold(0, 1, a, True)
    forward(1, 1, 2)
    for a in range(kvh):
        fold(0, 0, a, True)
        finish(0, a)
    forward(1, 2, lines)
    collect(1)
    for a in range(kvh):
        fold(1, 1, a, False)
    for a in range(kvh):
        finish(1, a)

    store_cross = pltpu.make_async_copy(out, cross_hbm, out_sem.at[1])
    store_cross.start()

    send_halo(0, "wait_send")
    send_halo(1, "wait_send")
    for b in range(2):
        for o in range(1, tpn):
            rs_copy(b, o).wait_send()
        own_cross(b, "wait_send")
        own_line(b, "wait_send")

        def sent(k, carry):
            @pl.when((k > z) if b == 1 else (k != z))
            def _():
                cross_copy(b, k).wait_send()

            return carry

        lax.fori_loop(0, lines, sent, 0)
    store_self.wait()
    store_cross.wait()


def per_device(n, tpn, q_self, k_self, v_self, window, key_weight, value_weight, q_cross):
    tokens, columns = q_self.shape
    stretch = tokens // 2
    heads = columns // HEAD_DIM
    layers = q_cross.shape[0]
    width = key_weight.shape[1] // tpn
    kvh = width // HEAD_DIM
    rows = layers * (heads // kvh) * stretch
    bf, f32 = jnp.bfloat16, jnp.float32
    any_space = pl.BlockSpec(memory_space=pl.ANY)
    dma = pltpu.SemaphoreType.DMA
    return pl.pallas_call(
        functools.partial(kernel, n, tpn),
        out_shape=(
            jax.ShapeDtypeStruct(q_self.shape, bf),
            jax.ShapeDtypeStruct(q_cross.shape, bf),
        ),
        in_specs=[pl.BlockSpec(memory_space=pltpu.SMEM)] + [any_space] * 6,
        out_specs=(any_space, any_space),
        scratch_shapes=[
            pltpu.VMEM(q_self.shape, bf),
            pltpu.VMEM((2, tokens, columns), bf),
            pltpu.VMEM((2, tokens, columns), bf),
            pltpu.VMEM(key_weight.shape, bf),
            pltpu.VMEM(value_weight.shape, bf),
            pltpu.VMEM(q_cross.shape, bf),
            pltpu.VMEM(q_self.shape, bf),
            pltpu.VMEM((2, tpn - 1, stretch, 2 * width), bf),
            pltpu.VMEM((2, tpn - 1, stretch, 2 * width), bf),
            pltpu.VMEM((2, stretch, 2 * width), f32),
            pltpu.VMEM((2, n, stretch, 2 * width), bf),
            pltpu.VMEM((2, kvh, rows, HEAD_DIM), bf),
            pltpu.VMEM((2, kvh, 1, rows), f32),
            pltpu.VMEM((2, kvh, 1, rows), f32),
            pltpu.VMEM((2, kvh, HEAD_DIM, rows), f32),
            pltpu.VMEM(q_cross.shape, bf),
            dma((8,)),
            dma((2, 2)),
            dma((2, 2)),
            dma((2, tpn - 1)),
            dma((2, tpn - 1)),
            dma((2, n // 2)),
            dma((2, n // 2)),
            dma((2, n)),
            dma((2,)),
        ],
        compiler_params=pltpu.CompilerParams(
            collective_id=0, has_side_effects=True, vmem_limit_bytes=60 * 2**20
        ),
    )(window, q_self, k_self, v_self, key_weight, value_weight, q_cross)


def solution(mesh):
    n, tpn = mesh.shape["ctx"], mesh.shape["tp"]
    placed = (
        P("ctx", "tp"),
        P("ctx", "tp"),
        P("ctx", "tp"),
        P(),
        P("tp", None),
        P("tp", None),
        P(None, "ctx", "tp"),
    )
    return jax.shard_map(
        functools.partial(per_device, n, tpn),
        mesh=mesh,
        in_specs=placed,
        out_specs=(P("ctx", "tp"), P(None, "ctx", "tp")),
        check_vma=False,
    )
```

time: 52.6 us -> 47.8 us (0.909)
  local copies, waits for them, and re-layouts: 7.63 us -> 3.54 us
  Pallas kernels: 44 us -> 43.4 us
    unnamed x14 -> x2, local copies, waits for them, and re-layouts: 7.63 us -> 3.54 us
    pallas_call x1, Pallas kernels: 44 us -> 43.4 us  [per_device(): pl.pallas_call(functools.partial(kernel, n, tpn), out_shape=(jax.ShapeDty...]
where the time goes in v2:
time: 47.8 us; the launch traced here: 47.6 us
  Pallas kernels  43.4 us (91%)
  local copies, waits for them, and re-layouts  3.54 us (7%)
  between operations  0.64 us (1%)
    pallas_call x1, Pallas kernels, per_device(): pl.pallas_call(functools.partial(kernel, n, tpn), out_shape=(jax.ShapeDty...  43.4 us
    unnamed x2, local copies, waits for them, and re-layouts  3.54 us

profile of v2, /device:TPU:0, one launch (start us, length us, event | category | flops | bytes accessed | tf_op | source)
XLA Modules:
  0.0 47.6 jit_solution(15512156162699824652)
XLA Ops:
  0.6 43.4 %shard_map.86 = (bf16[128,1024]{1,0:T(8,128)(2,1)}, bf16[2,128,1024]{2,1,0:T(8,128)(2,1)}) custom-call(s32[32]{0:T(128)} %window.1, bf16[128,1024]{1,0:T(8,128)(2,1)} %q_hbm.1, bf16[128,1024]{1,0:T(8,128)(2,1)} %k_hbm.1, bf16[128,1024]{1,0:T(8,128)(2,1)} %v_hbm.1, bf16[1024,1024]{1,0:T(8,128)(2,1)} %kw_hbm.1, bf16[1024,1024]{1,0:T(8,128)(2,1)} %vw_hbm.1, ...), custom_call_target="tpu_custom_call" | custom-call | tf_op jit(solution)/shard_map/pallas_call | solution.py:389
  44.1 1.7 %copy.11 = bf16[128,1024]{1,0:T(8,128)(2,1)} copy(bf16[128,1024]{1,0:T(8,128)(2,1)} %get-tuple-element.4) | data formatting | bytes 524288
  45.7 1.9 %copy.12 = bf16[2,128,1024]{2,1,0:T(8,128)(2,1)} copy(bf16[2,128,1024]{2,1,0:T(8,128)(2,1)} %get-tuple-element.5) | data formatting | bytes 1048576
